TPU v7x, 32 devices: a whole 2x2x4 slice. The times are simulated.
32 devices in a mesh: wide: 16 (over z, x, core), heads: 2 (over y).
Axes of the slice: x: 2, y: 2, z: 4, core: 2. Of those that a mesh axis runs over, the one named last changes fastest.
Arguments:
- inputs: bfloat16 [32768, 1280], P('wide'), may hold values from -6 to 6
- segment_ids: int32 [32768], P('wide'), may hold values from 0 to 4095, never falling along the last dimension, each value on 1 to 16 neighbouring positions
- cotangent: bfloat16 [32768, 1280], P('wide'), may hold values from -6 to 6
- w_query: bfloat16 [1280, 1280], P('wide', 'heads'), may hold values from -0.15625 to 0.15625
- w_key: bfloat16 [1280, 1280], P('wide', 'heads'), may hold values from -0.15625 to 0.15625
- w_value: bfloat16 [1280, 1280], P('wide', 'heads'), may hold values from -0.15625 to 0.15625
- w_out: bfloat16 [1280, 1280], P('heads', 'wide'), may hold values from -0.3125 to 0.3125
- w_up: bfloat16 [1280, 1280], P('wide', 'heads'), may hold values from -0.15625 to 0.15625
- w_down: bfloat16 [1280, 1280], P('heads', 'wide'), may hold values from -0.25 to 0.25
- b_query: float32 [1280], replicated, may hold values from -3 to 3
- b_value: float32 [1280], replicated, may hold values from -3 to 3
- b_out: float32 [1280], replicated, may hold values from -3 to 3
- b_up: float32 [1280], replicated, may hold values from -3 to 3
- b_down: float32 [1280], replicated, may hold values from -3 to 3
- dim_scale: float32 [80], replicated, may hold values from -1 to 1.5
- gain_attn: float32 [1280], replicated, may hold values from 0.5 to 1.5
- gain_mlp: float32 [1280], replicated, may hold values from 0.5 to 1.5
Outputs:
- output: bfloat16 [32768, 1280], P(('wide', 'heads'))
- input_grad: float32 [32768, 1280], P(('wide', 'heads'))
- grad_w_query: float32 [1280, 1280], P('wide', 'heads')
- grad_w_key: float32 [1280, 1280], P('wide', 'heads')
- grad_w_value: float32 [1280, 1280], P('wide', 'heads')
- grad_w_out: float32 [1280, 1280], P('heads', 'wide')
- grad_w_up: float32 [1280, 1280], P('wide', 'heads')
- grad_w_down: float32 [1280, 1280], P('heads', 'wide')
- grad_b_query: float32 [1280], replicated
- grad_b_value: float32 [1280], replicated
- grad_b_out: float32 [1280], replicated
- grad_b_up: float32 [1280], replicated
- grad_b_down: float32 [1280], replicated
- grad_dim_scale: float32 [80], replicated
- grad_gain_attn: float32 [1280], replicated
- grad_gain_mlp: float32 [1280], replicated
Inputs may be any that keep to these rules, and one draw needn't show every extreme that they name: `segment_ids`: segment numbers never fall along the tokens; a segment has 1 to 16 tokens.
All inputs are finite; a program needn't handle non-finite values.
Results may differ from a plain program's by a relative error of at most 0.015.
Values may be sent and summed in bfloat16 or wider, within the bound.
A program may use at most 192 MiB of HBM per device.

v0:
```python
import math
import jax
import jax.numpy as jnp
from jax import lax
from jax.sharding import PartitionSpec as P

DH = 80
PATCHES = 16
eps = 1e-06
query_base = 1.442695041


def dot_plain(left, right):
    return jnp.dot(left, right, preferred_element_type=jnp.float32)


def dot_left(left, right):
    return lax.dot_general(
        left, right, (((0,), (0,)), ((), ())), preferred_element_type=jnp.float32
    )


def dot_right(left, right):
    return lax.dot_general(
        left, right, (((1,), (1,)), ((), ())), preferred_element_type=jnp.float32
    )


def inverse_rms(values):
    return lax.rsqrt(jnp.mean(values * values, axis=-1, keepdims=True) + eps)


def norm_back(values, gain_vec, grad_in):
    factor = inverse_rms(values)
    inner = jnp.mean(grad_in * gain_vec * values, axis=-1, keepdims=True)
    grad_out = factor * gain_vec * grad_in - values * factor * factor * factor * inner
    return (grad_out, jnp.sum(grad_in * values * factor, axis=0))


def tile_mask(seg_tiles, tile_len):
    position = jnp.arange(tile_len)
    same_row = position[:, None] // PATCHES == position[None, :] // PATCHES
    causal = position[:, None] >= position[None, :]
    same_seg = seg_tiles[:, :, None] == seg_tiles[:, None, :]
    return (same_seg & (same_row & causal)[None])[:, None]


def masked_scores(query_tiles, key_tiles, allowed):
    scores = jnp.einsum(
        "bqhe,bkhe->bhqk", query_tiles, key_tiles, preferred_element_type=jnp.float32
    )
    return jnp.where(allowed, scores, -1e30)


def place_part(vector, length, offset):
    return lax.dynamic_update_slice_in_dim(jnp.zeros((length,), jnp.float32), vector, offset, 0)


def shards(
    inputs,
    segment_ids,
    cotangent,
    w_query,
    w_key,
    w_value,
    w_out,
    w_up,
    w_down,
    b_query,
    b_value,
    b_out,
    b_up,
    b_down,
    dim_scale,
    gain_attn,
    gain_mlp,
):
    tok_rows = inputs.shape[0]
    head_groups = lax.axis_size("heads")
    head_index = lax.axis_index("heads")
    half_rows = tok_rows // head_groups
    local_hd = w_query.shape[1]
    local_ff = w_up.shape[1]
    local_heads = local_hd // DH
    tile_len = min(128, tok_rows)
    tile_count = tok_rows // tile_len
    row_start = head_index * half_rows
    input_full = inputs.astype(jnp.float32)
    input_half = lax.dynamic_slice_in_dim(input_full, row_start, half_rows, 0)
    cot_half = lax.dynamic_slice_in_dim(cotangent, row_start, half_rows, 0)
    grad_half = cot_half.astype(jnp.float32)
    bias_query = lax.dynamic_slice_in_dim(b_query, head_index * local_hd, local_hd, 0)
    bias_value = lax.dynamic_slice_in_dim(b_value, head_index * local_hd, local_hd, 0)
    bias_up = lax.dynamic_slice_in_dim(b_up, head_index * local_ff, local_ff, 0)
    scale_const = query_base / math.sqrt(DH)
    query_scale = scale_const * jax.nn.softplus(dim_scale)
    tile_shape = (tile_count, tile_len, local_heads, DH)
    query_full, key_full, value_full, out_full = (
        lax.all_gather(w_query, "wide", axis=0, tiled=True),
        lax.all_gather(w_key, "wide", axis=0, tiled=True),
        lax.all_gather(w_value, "wide", axis=0, tiled=True),
        lax.all_gather(w_out, "wide", axis=1, tiled=True),
    )
    normed_one = (input_full * inverse_rms(input_full) * gain_attn).astype(jnp.bfloat16)
    query_proj = dot_plain(normed_one, query_full) + bias_query
    query_tiles = (query_proj.reshape(tile_shape) * query_scale).astype(jnp.bfloat16)
    key_tiles = dot_plain(normed_one, key_full).astype(jnp.bfloat16).reshape(tile_shape)
    value_tiles = (
        (dot_plain(normed_one, value_full) + bias_value).astype(jnp.bfloat16).reshape(tile_shape)
    )
    allowed = tile_mask(segment_ids.reshape(tile_count, tile_len), tile_len)
    scores = masked_scores(query_tiles, key_tiles, allowed)
    row_max = jnp.max(scores, axis=-1, keepdims=True)
    exp_scores = jnp.exp(scores - row_max)
    row_total = jnp.sum(exp_scores, axis=-1, keepdims=True)
    attn_probs = exp_scores / row_total
    log_total = row_max + jnp.log(row_total)
    attended = jnp.einsum(
        "bhqk,bkhe->bqhe",
        attn_probs.astype(jnp.bfloat16),
        value_tiles,
        preferred_element_type=jnp.float32,
    )
    attended = attended.reshape(tok_rows, local_hd).astype(jnp.bfloat16)
    up_full, down_full = (
        lax.all_gather(w_up, "wide", axis=0, tiled=True),
        lax.all_gather(w_down, "wide", axis=1, tiled=True),
    )
    attn_half = lax.psum_scatter(
        dot_plain(attended, out_full), "heads", scatter_dimension=0, tiled=True
    )
    residual = input_half + attn_half + b_out
    normed_half = (residual * inverse_rms(residual) * gain_mlp).astype(jnp.bfloat16)
    normed_two = lax.all_gather(normed_half, "heads", axis=0, tiled=True)
    up_proj = dot_plain(normed_two, up_full) + bias_up
    activated = jax.nn.gelu(up_proj).astype(jnp.bfloat16)
    mlp_half = lax.psum_scatter(
        dot_plain(activated, down_full).astype(jnp.bfloat16),
        "heads",
        scatter_dimension=0,
        tiled=True,
    ).astype(jnp.float32)
    output = (residual + mlp_half + b_down).astype(jnp.bfloat16)
    up_full, down_full = (
        lax.all_gather(w_up, "wide", axis=0, tiled=True),
        lax.all_gather(w_down, "wide", axis=1, tiled=True),
    )
    grad_down = dot_left(activated, cotangent)
    grad_act = dot_right(cotangent, down_full)
    unused_value, gelu_pull = jax.vjp(jax.nn.gelu, up_proj)
    grad_up_proj = gelu_pull(grad_act)[0].astype(jnp.bfloat16)
    grad_up = dot_left(normed_two, grad_up_proj)
    bias_up_term = place_part(
        jnp.sum(grad_up_proj.astype(jnp.float32), axis=0), b_up.shape[0], head_index * local_ff
    )
    grad_norm_two = lax.psum_scatter(
        dot_right(grad_up_proj, up_full).astype(jnp.bfloat16),
        "heads",
        scatter_dimension=0,
        tiled=True,
    ).astype(jnp.float32)
    back_two, grad_gain_two = norm_back(residual, gain_mlp, grad_norm_two)
    grad_resid = grad_half + back_two
    branch_half = grad_resid.astype(jnp.bfloat16)
    query_full, key_full, value_full, out_full = (
        lax.all_gather(w_query, "wide", axis=0, tiled=True),
        lax.all_gather(w_key, "wide", axis=0, tiled=True),
        lax.all_gather(w_value, "wide", axis=0, tiled=True),
        lax.all_gather(w_out, "wide", axis=1, tiled=True),
    )
    grad_branch = lax.all_gather(branch_half, "heads", axis=0, tiled=True)
    grad_out = dot_left(attended, grad_branch)
    grad_attended = dot_right(grad_branch, out_full).astype(jnp.bfloat16).reshape(tile_shape)
    probs_again = jnp.exp(masked_scores(query_tiles, key_tiles, allowed) - log_total)
    grad_probs = jnp.einsum(
        "bqhe,bkhe->bhqk", grad_attended, value_tiles, preferred_element_type=jnp.float32
    )
    inner = jnp.sum(probs_again * grad_probs, axis=-1, keepdims=True)
    grad_scores = (probs_again * (grad_probs - inner)).astype(jnp.bfloat16)
    grad_qs = jnp.einsum(
        "bhqk,bkhe->bqhe", grad_scores, key_tiles, preferred_element_type=jnp.float32
    )
    grad_key_proj = jnp.einsum(
        "bhqk,bqhe->bkhe", grad_scores, query_tiles, preferred_element_type=jnp.float32
    )
    grad_key_proj = grad_key_proj.reshape(tok_rows, local_hd).astype(jnp.bfloat16)
    grad_value_proj = jnp.einsum(
        "bhqk,bqhe->bkhe",
        probs_again.astype(jnp.bfloat16),
        grad_attended,
        preferred_element_type=jnp.float32,
    )
    grad_value_proj = grad_value_proj.reshape(tok_rows, local_hd).astype(jnp.bfloat16)
    grad_dim = (
        jnp.sum(grad_qs * query_proj.reshape(tile_shape), axis=(0, 1, 2))
        * scale_const
        * jax.nn.sigmoid(dim_scale)
    )
    grad_query_proj = (grad_qs * query_scale).reshape(tok_rows, local_hd).astype(jnp.bfloat16)
    grad_query = dot_left(normed_one, grad_query_proj)
    grad_key = dot_left(normed_one, grad_key_proj)
    grad_value = dot_left(normed_one, grad_value_proj)
    sum_query = jnp.sum(grad_query_proj.astype(jnp.float32), axis=0)
    sum_value = jnp.sum(grad_value_proj.astype(jnp.float32), axis=0)
    norm_terms = (
        dot_right(grad_query_proj, query_full)
        + dot_right(grad_key_proj, key_full)
        + dot_right(grad_value_proj, value_full)
    )
    grad_norm_one = lax.psum_scatter(
        norm_terms.astype(jnp.bfloat16), "heads", scatter_dimension=0, tiled=True
    ).astype(jnp.float32)
    back_one, grad_gain_one = norm_back(input_half, gain_attn, grad_norm_one)
    input_grad = grad_resid + back_one
    grad_up_w, grad_down_w = (
        lax.psum_scatter(grad_up, "wide", scatter_dimension=0, tiled=True),
        lax.psum_scatter(grad_down, "wide", scatter_dimension=1, tiled=True),
    )
    grad_query_w, grad_key_w, grad_value_w, grad_out_w = (
        lax.psum_scatter(grad_query, "wide", scatter_dimension=0, tiled=True),
        lax.psum_scatter(grad_key, "wide", scatter_dimension=0, tiled=True),
        lax.psum_scatter(grad_value, "wide", scatter_dimension=0, tiled=True),
        lax.psum_scatter(grad_out, "wide", scatter_dimension=1, tiled=True),
    )
    small_sums = lax.psum(
        (
            grad_gain_one,
            grad_gain_two,
            jnp.sum(grad_resid, axis=0),
            jnp.sum(grad_half, axis=0),
            grad_dim,
            place_part(sum_query, b_query.shape[0], head_index * local_hd),
            place_part(sum_value, b_value.shape[0], head_index * local_hd),
            bias_up_term,
        ),
        ("wide", "heads"),
    )
    (
        gain_one_sum,
        gain_two_sum,
        bias_out_sum,
        bias_down_sum,
        dim_sum,
        bias_query_sum,
        bias_value_sum,
        bias_up_sum,
    ) = small_sums
    return (
        output,
        input_grad,
        grad_query_w,
        grad_key_w,
        grad_value_w,
        grad_out_w,
        grad_up_w,
        grad_down_w,
        bias_query_sum,
        bias_value_sum,
        bias_out_sum,
        bias_up_sum,
        bias_down_sum,
        dim_sum,
        gain_one_sum,
        gain_two_sum,
    )


def solution(mesh):
    return jax.shard_map(
        shards,
        mesh=mesh,
        in_specs=(
            P("wide", None),
            P("wide"),
            P("wide", None),
            P("wide", "heads"),
            P("wide", "heads"),
            P("wide", "heads"),
            P("heads", "wide"),
            P("wide", "heads"),
            P("heads", "wide"),
            P(),
            P(),
            P(),
            P(),
            P(),
            P(),
            P(),
            P(),
        ),
        out_specs=(
            P(("wide", "heads"), None),
            P(("wide", "heads"), None),
            P("wide", "heads"),
            P("wide", "heads"),
            P("wide", "heads"),
            P("heads", "wide"),
            P("wide", "heads"),
            P("heads", "wide"),
            P(),
            P(),
            P(),
            P(),
            P(),
            P(),
            P(),
            P(),
        ),
        check_vma=False,
    )
```

profile of v0, /device:TPU:0, one launch (start us, length us, event | category | flops | bytes accessed | tf_op | source)
XLA Modules:
  0.0 1287.7 jit_solution(7532887947847363733)
XLA Ops:
  12.3 3.6 multiply_reduce_fusion
  16.3 36.5 %all-gather.9.cloned.1.call-done = bf16[1280,640]{1,0:T(8,128)(2,1)} async-done(((bf16[80,640]{1,0:T(8,128)(2,1)}), bf16[1280,640]{1,0:T(8,128)(2,1)}) %all-gather.9.cloned.1.call-update) | async-done | bytes 1638416 | tf_op jit(solution)/shard_map/all_gather | solution.py:101
  52.9 7.4 add_convert_fusion.2
  60.2 33.6 %all-gather.11.cloned.1.call-done = bf16[1280,640]{1,0:T(8,128)(2,1)} async-done(((bf16[80,640]{1,0:T(8,128)(2,1)}), bf16[1280,640]{1,0:T(8,128)(2,1)}) %all-gather.11.cloned.1.call-update) | async-done | bytes 1638416 | tf_op jit(solution)/shard_map/all_gather | solution.py:99
  93.9 9.7 convolution_add_fusion
  103.5 31.4 %all-gather.13.cloned.1.call-done = bf16[1280,640]{1,0:T(8,128)(2,1)} async-done(((bf16[80,640]{1,0:T(8,128)(2,1)}), bf16[1280,640]{1,0:T(8,128)(2,1)}) %all-gather.13.cloned.1.call-update) | async-done | bytes 1638416 | tf_op jit(solution)/shard_map/all_gather | solution.py:100
  134.9 9.3 convolution_convert_fusion.3
  144.2 5.2 reshape.228
  149.4 6.3 copy.50
  155.7 5.2 reshape.230
  160.9 6.1 copy.49
  167.0 9.5 reshape.229
  176.4 8.3 copy.47
  184.7 4.5 select_reduce_fusion
  189.2 2.4 fusion
  192.8 2.4 convert_bitcast_fusion.1
  197.0 10.0 fusion.42
  207.7 7.6 convert_element_type.111
  215.3 112.8 %reduce-scatter.11.cloned.1.call-done = f32[1024,1280]{1,0:T(8,128)} async-done(((f32[2048,1280]{1,0:T(8,128)}), f32[1024,1280]{1,0:T(8,128)}) %reduce-scatter.11.cloned.1.call-update) | async-done | bytes 5242896 | tf_op jit(solution)/shard_map/reduce_scatter | solution.py:129
  328.2 5.8 multiply_reduce_fusion.3
  334.0 2.3 copy-done.1
  336.3 2.0 multiply_convert_fusion.3
  339.2 30.9 %all-gather.19.cloned.1.call-done = bf16[1280,640]{1,0:T(8,128)(2,1)} async-done(((bf16[80,640]{1,0:T(8,128)(2,1)}), bf16[1280,640]{1,0:T(8,128)(2,1)}) %all-gather.19.cloned.1.call-update) | async-done | bytes 1638416 | tf_op jit(solution)/shard_map/all_gather | solution.py:126
  370.1 69.6 %all-gather.17.cloned.1.call-done = bf16[2048,1280]{1,0:T(8,128)(2,1)} async-done(((bf16[1024,1280]{1,0:T(8,128)(2,1)}), bf16[2048,1280]{1,0:T(8,128)(2,1)}) %all-gather.17.cloned.1.call-update) | async-done | bytes 5242896 | tf_op jit(solution)/shard_map/all_gather | solution.py:134
  439.8 9.5 fusion.64
  449.3 32.6 %all-gather.21.cloned.1.call-done = bf16[640,1280]{0,1:T(8,128)(2,1)} async-done(((bf16[640,80]{0,1:T(8,128)(2,1)}), bf16[640,1280]{0,1:T(8,128)(2,1)}) %all-gather.21.cloned.1.call-update) | async-done | bytes 1638416 | tf_op jit(solution)/shard_map/all_gather | solution.py:127
  481.9 10.0 convert_reduce_fusion.1
  493.4 6.0 convolution_convert_fusion
  500.8 10.5 convolution_convert_fusion.1
  511.4 52.7 %reduce-scatter.15.cloned.1.call-done = bf16[1024,1280]{1,0:T(8,128)(2,1)} async-done(((bf16[2048,1280]{1,0:T(8,128)(2,1)}), bf16[1024,1280]{1,0:T(8,128)(2,1)}) %reduce-scatter.15.cloned.1.call-update) | async-done | bytes 2621456 | tf_op jit(solution)/shard_map/reduce_scatter | solution.py:156
  564.1 5.0 fusion.13
  569.2 63.0 %reduce-scatter.13.cloned.1.call-done = bf16[1024,1280]{1,0:T(8,128)(2,1)} async-done(((bf16[2048,1280]{1,0:T(8,128)(2,1)}), bf16[1024,1280]{1,0:T(8,128)(2,1)}) %reduce-scatter.13.cloned.1.call-update) | async-done | bytes 2621456 | tf_op jit(solution)/shard_map/reduce_scatter | solution.py:137
  632.1 6.8 fusion.62
  638.9 2.4 copy-done.2
  641.3 1.8 convert_element_type.129
  643.7 68.2 %all-gather.23.cloned.1.call-done = bf16[2048,1280]{1,0:T(8,128)(2,1)} async-done(((bf16[1024,1280]{1,0:T(8,128)(2,1)}), bf16[2048,1280]{1,0:T(8,128)(2,1)}) %all-gather.23.cloned.1.call-update) | async-done | bytes 5242896 | tf_op jit(solution)/shard_map/all_gather | solution.py:171
  711.9 7.2 convolution_convert_fusion.2
  719.2 5.2 reshape.231
  724.4 6.1 copy.54
  730.5 8.0 convert_reduce_fusion.2
  738.6 10.1 multiply_reduce_fusion.1
  748.6 5.4 multiply_convert_fusion.1
  754.1 1.8 convert_reduce_fusion.3
  755.9 3.1 convert_bitcast_fusion
  759.0 1.7 copy.63
  764.1 7.8 fusion.34
  771.9 8.1 fusion.38
  780.0 11.3 add_convert_fusion
  791.5 9.4 fusion.65
  801.3 10.3 fusion.60
  811.7 9.2 fusion.40
  821.2 10.1 fusion.36
  831.4 9.8 fusion.32
  841.5 9.1 fusion.29
  851.7 5.5 reduce-scatter.17.cloned.1.call-done
  857.2 5.0 fusion.19
  862.3 41.1 %all-reduce = (f32[1280]{0:T(1024)}, f32[1280]{0:T(1024)}, f32[1280]{0:T(1024)}, f32[1280]{0:T(1024)}, f32[1280]{0:T(1024)}, /*index=5*/f32[80]{0:T(128)}, f32[1280]{0:T(1024)}, f32[1280]{0:T(1024)}) all-reduce(f32[1280]{0:T(1024)S(1)} %dynamic_update_slice.9, ...), channel_id=1, replica_groups=mesh['wide'=16,'heads'=2] {'wide','heads'}, use_global_device_ids=true, to_apply=%region_19.20 | all-reduce | flops 9040 | bytes 72320 | tf_op jit(solution)/shard_map/psum | solution.py:225
  903.4 6.5 fusion.15
  909.9 19.7 %reduce-scatter.27.cloned.1.call-done = f32[80,640]{1,0:T(8,128)} async-done(((f32[1280,640]{1,0:T(8,128)}), f32[80,640]{1,0:T(8,128)}) %reduce-scatter.27.cloned.1.call-update) | async-done | bytes 204816 | tf_op jit(solution)/shard_map/reduce_scatter | solution.py:216
  929.6 70.0 %reduce-scatter.29.cloned.1.call-done = f32[640,80]{0,1:T(8,128)} async-done(((f32[640,1280]{0,1:T(8,128)}), f32[640,80]{0,1:T(8,128)}) %reduce-scatter.29.cloned.1.call-update) | async-done | bytes 204816 | tf_op jit(solution)/shard_map/reduce_scatter | solution.py:217
  999.6 70.5 %reduce-scatter.25.cloned.1.call-done = f32[640,80]{0,1:T(8,128)} async-done(((f32[640,1280]{0,1:T(8,128)}), f32[640,80]{0,1:T(8,128)}) %reduce-scatter.25.cloned.1.call-update) | async-done | bytes 204816 | tf_op jit(solution)/shard_map/reduce_scatter | solution.py:223
  1070.1 70.0 %reduce-scatter.19.cloned.1.call-done = f32[80,640]{1,0:T(8,128)} async-done(((f32[1280,640]{1,0:T(8,128)}), f32[80,640]{1,0:T(8,128)}) %reduce-scatter.19.cloned.1.call-update) | async-done | bytes 204816 | tf_op jit(solution)/shard_map/reduce_scatter | solution.py:220
  1140.2 70.4 %reduce-scatter.21.cloned.1.call-done = f32[80,640]{1,0:T(8,128)} async-done(((f32[1280,640]{1,0:T(8,128)}), f32[80,640]{1,0:T(8,128)}) %reduce-scatter.21.cloned.1.call-update) | async-done | bytes 204816 | tf_op jit(solution)/shard_map/reduce_scatter | solution.py:221
  1210.6 70.0 %reduce-scatter.23.cloned.1.call-done = f32[80,640]{1,0:T(8,128)} async-done(((f32[1280,640]{1,0:T(8,128)}), f32[80,640]{1,0:T(8,128)}) %reduce-scatter.23.cloned.1.call-update) | async-done | bytes 204816 | tf_op jit(solution)/shard_map/reduce_scatter | solution.py:222
  (130 shorter events, 19.1 us)
Async XLA Ops:
  7.2 8.8 copy-start.17
  7.2 45.7 %copy-start.15 = (f32[1280]{0:T(1024)S(1)}, f32[1280]{0:T(1024)}, u32[]{:S(2)}) copy-start(f32[1280]{0:T(1024)} %param.32) | copy-start | bytes 15364
  7.2 45.7 %all-gather.9.cloned.1.call-start = ((), (), s32[]{:S(2)}) async-start(), calls=%async_computation.10 | async-start | bytes 1740800 | tf_op jit(solution)/shard_map/all_gather | solution.py:101
  7.9 85.9 %all-gather.11.cloned.1.call-start = ((), (), s32[]{:S(2)}) async-start(), calls=%async_computation.11 | async-start | bytes 1740800 | tf_op jit(solution)/shard_map/all_gather | solution.py:99
  8.7 126.2 %all-gather.13.cloned.1.call-start = ((), (), s32[]{:S(2)}) async-start(), calls=%async_computation.12 | async-start | bytes 1740800 | tf_op jit(solution)/shard_map/all_gather | solution.py:100
  9.4 187.6 %all-gather.15.cloned.1.call-start = ((), (), s32[]{:S(2)}) async-start(), calls=%async_computation.13 | async-start | bytes 1740800 | tf_op jit(solution)/shard_map/all_gather | solution.py:102
  10.0 318.2 %reduce-scatter.11.cloned.1.call-start = ((), (), s32[]{:S(2)}) async-start(), calls=%async_computation.14 | async-start | bytes 15728640 | tf_op jit(solution)/shard_map/reduce_scatter | solution.py:129
  15.9 119.0 %copy-start.21 = (f32[2048]{0:T(1024)}, f32[2048]{0:T(1024)S(1)}, u32[]{:S(2)}) copy-start(f32[2048]{0:T(1024)S(1)} %add_rsqrt_fusion) | copy-start | bytes 24580
  149.4 6.3 copy-start.12
  167.0 17.7 %copy-start.3 = (bf16[16,128,8,80]{1,3,2,0:T(8,128)(2,1)}, bf16[16,128,8,80]{1,3,2,0:T(8,128)(2,1)S(1)}, u32[]{:S(2)}) copy-start(bf16[16,128,8,80]{1,3,2,0:T(8,128)(2,1)S(1)} %copy.49) | copy-start | bytes 7864324
  189.1 6.1 copy-start
  189.1 3.7 copy-start.7
  197.0 10.0 copy-start.9
  207.0 163.1 %all-gather.19.cloned.1.call-start = ((), (), s32[]{:S(2)}) async-start(), calls=%async_computation.16 | async-start | bytes 1740800 | tf_op jit(solution)/shard_map/all_gather | solution.py:126
  207.6 120.5 %copy-start.19 = (f32[1280]{0:T(1024)S(1)}, f32[1280]{0:T(1024)}, u32[]{:S(2)}) copy-start(f32[1280]{0:T(1024)} %param.28) | copy-start | bytes 15364
  207.6 232.1 %all-gather.17.cloned.1.call-start = ((), (), s32[]{:S(2)}) async-start(), calls=%async_computation.15 | async-start | bytes 7864320 | tf_op jit(solution)/shard_map/all_gather | solution.py:134
  215.3 121.0 %copy-start.14 = (f32[1280]{0:T(1024)S(1)}, f32[1280]{0:T(1024)}, u32[]{:S(2)}) copy-start(f32[1280]{0:T(1024)} %param.33) | copy-start | bytes 15364
  333.9 2.3 copy-start.1
  336.3 2.8 copy-start.23
  338.3 143.6 %all-gather.21.cloned.1.call-start = ((), (), s32[]{:S(2)}) async-start(), calls=%async_computation.17 | async-start | bytes 1740800 | tf_op jit(solution)/shard_map/all_gather | solution.py:127
  339.1 225.1 %reduce-scatter.15.cloned.1.call-start = ((), (), s32[]{:S(2)}) async-start(), calls=%async_computation.19 | async-start | bytes 7864320 | tf_op jit(solution)/shard_map/reduce_scatter | solution.py:156
  449.3 44.1 %copy-start.26 = (bf16[1280,640]{1,0:T(8,128)(2,1)S(1)}, bf16[1280,640]{1,0:T(8,128)(2,1)}, u32[]{:S(2)}) copy-start(bf16[1280,640]{1,0:T(8,128)(2,1)} %all-gather.19.cloned.1.call-done) | copy-start | bytes 4915204
  491.9 1.5 copy-start.29
  499.4 1.4 copy-start.27
  499.4 132.7 %reduce-scatter.13.cloned.1.call-start = ((), (), s32[]{:S(2)}) async-start(), calls=%async_computation.18 | async-start | bytes 7864320 | tf_op jit(solution)/shard_map/reduce_scatter | solution.py:137
  511.4 120.8 %copy-start.20 = (f32[1280]{0:T(1024)S(1)}, f32[1280]{0:T(1024)}, u32[]{:S(2)}) copy-start(f32[1280]{0:T(1024)} %param.30) | copy-start | bytes 15364
  511.4 200.5 %all-gather.23.cloned.1.call-start = ((), (), s32[]{:S(2)}) async-start(), calls=%async_computation.20 | async-start | bytes 7864320 | tf_op jit(solution)/shard_map/all_gather | solution.py:171
  564.1 68.0 %copy-start.8 = (bf16[1024,1280]{1,0:T(8,128)(2,1)S(1)}, bf16[1024,1280]{1,0:T(8,128)(2,1)}, u32[]{:S(2)}) copy-start(bf16[1024,1280]{1,0:T(8,128)(2,1)} %reduce-scatter.15.cloned.1.call-done) | copy-start | bytes 7864324
  638.9 2.4 copy-start.2
  643.2 214.0 %reduce-scatter.17.cloned.1.call-start = ((), (), s32[]{:S(2)}) async-start(), calls=%async_computation.21 | async-start | bytes 7864320 | tf_op jit(solution)/shard_map/reduce_scatter | solution.py:210
  730.5 18.1 %slice-start = ((s8[8388608]{0:T(1024)(128)(4,1)}), s8[4194304]{0:T(1024)(128)(4,1)S(1)}, s32[]{:S(2)}) async-start(s8[8388608]{0:T(1024)(128)(4,1)} %bitcast.78), calls=%async_computation.28 | async-start | bytes 8388608
  730.5 23.5 %slice-start.2 = ((s8[5242880]{0:T(1024)(128)(4,1)}), s8[4194304]{0:T(1024)(128)(4,1)S(1)}, s32[]{:S(2)}) async-start(s8[5242880]{0:T(1024)(128)(4,1)} %bitcast.80), calls=%async_computation.30 | async-start | bytes 8388608
  738.6 10.1 slice-start.1
  738.6 15.5 %slice-start.3 = ((s8[5242880]{0:T(1024)(128)(4,1)}), s8[1048576]{0:T(1024)(128)(4,1)S(1)}, s32[]{:S(2)}) async-start(s8[5242880]{0:T(1024)(128)(4,1)} %bitcast.80), calls=%async_computation.31 | async-start | bytes 2097152
  748.6 5.4 copy-start.4
  755.9 3.1 copy-start.6
  760.7 3.4 copy-start.25
  762.4 9.5 copy-start.10
  764.1 7.8 copy-start.11
  764.1 7.8 copy-start.24
  771.9 8.1 copy-start.13
  791.4 138.2 %reduce-scatter.27.cloned.1.call-start = ((), (), s32[]{:S(2)}) async-start(), calls=%async_computation.26 | async-start | bytes 3481600 | tf_op jit(solution)/shard_map/reduce_scatter | solution.py:216
  800.9 198.7 %reduce-scatter.29.cloned.1.call-start = ((), (), s32[]{:S(2)}) async-start(), calls=%async_computation.27 | async-start | bytes 3481600 | tf_op jit(solution)/shard_map/reduce_scatter | solution.py:217
  811.6 9.6 copy-start.16
  811.6 9.6 copy-start.22
  811.7 258.5 %reduce-scatter.25.cloned.1.call-start = ((), (), s32[]{:S(2)}) async-start(), calls=%async_computation.25 | async-start | bytes 3481600 | tf_op jit(solution)/shard_map/reduce_scatter | solution.py:223
  821.0 319.2 %reduce-scatter.19.cloned.1.call-start = ((), (), s32[]{:S(2)}) async-start(), calls=%async_computation.22 | async-start | bytes 3481600 | tf_op jit(solution)/shard_map/reduce_scatter | solution.py:220
  831.4 379.3 %reduce-scatter.21.cloned.1.call-start = ((), (), s32[]{:S(2)}) async-start(), calls=%async_computation.23 | async-start | bytes 3481600 | tf_op jit(solution)/shard_map/reduce_scatter | solution.py:221
  841.2 9.4 copy-start.18
  841.2 10.5 copy-start.28
  841.2 439.4 %reduce-scatter.23.cloned.1.call-start = ((), (), s32[]{:S(2)}) async-start(), calls=%async_computation.24 | async-start | bytes 3481600 | tf_op jit(solution)/shard_map/reduce_scatter | solution.py:222
  857.2 46.1 %copy-start.5 = (bf16[1024,1280]{1,0:T(8,128)(2,1)S(1)}, bf16[1024,1280]{1,0:T(8,128)(2,1)}, u32[]{:S(2)}) copy-start(bf16[1024,1280]{1,0:T(8,128)(2,1)} %reduce-scatter.17.cloned.1.call-done) | copy-start | bytes 7864324
Sparse Core Ops, SparseCore 0:
  10.2 42.6 all-gather.8
  55.0 38.8 all-gather.10
  96.1 38.8 all-gather.12
  136.9 38.8 all-gather.14
  207.2 120.9 reduce-scatter.10
  330.2 39.9 all-gather.18
  372.3 67.4 all-gather.16
  441.9 39.9 all-gather.20
  499.5 64.5 reduce-scatter.14
  566.4 65.6 reduce-scatter.12
  643.3 68.5 all-gather.22
  791.5 65.6 reduce-scatter.16
  862.1 67.4 reduce-scatter.26
  933.9 65.7 reduce-scatter.28
  1004.4 65.7 reduce-scatter.24
  1074.4 65.7 reduce-scatter.18
  1144.9 65.6 reduce-scatter.20
  1214.9 65.7 reduce-scatter.22
where the time goes:
time: 1300 us; the launch traced here: 1290 us
  waiting for transfers between devices  912 us (70%)
  matrix products  195 us (15%)
  local copies, waits for them, and re-layouts  70.2 us (5%)
  other arithmetic  53.1 us (4%)
  blocking collectives  41.1 us (3%)
  between operations  15 us (1%)
    reduce_scatter x1, waiting for transfers between devices, shards(): lax.psum_scatter(dot_plain(attended, out_full), 'heads', scatter_dimensio...  113 us
    reduce_scatter x1, waiting for transfers between devices, shards(): lax.psum_scatter(grad_out, 'wide', scatter_dimension=1, tiled=True)  70.5 us
    reduce_scatter x1, waiting for transfers between devices, shards(): lax.psum_scatter(grad_key, 'wide', scatter_dimension=0, tiled=True)  70.4 us
    reduce_scatter x1, waiting for transfers between devices, shards(): lax.psum_scatter(grad_value, 'wide', scatter_dimension=0, tiled=True)  70 us
    reduce_scatter x1, waiting for transfers between devices, shards(): lax.psum_scatter(grad_query, 'wide', scatter_dimension=0, tiled=True)  70 us
    reduce_scatter x1, waiting for transfers between devices, shards(): lax.psum_scatter(grad_down, 'wide', scatter_dimension=1, tiled=True)  70 us
    all_gather x1, waiting for transfers between devices, shards(): normed_two = lax.all_gather(normed_half, 'heads', axis=0, tiled=True)  69.6 us
    all_gather x1, waiting for transfers between devices, shards(): grad_branch = lax.all_gather(branch_half, 'heads', axis=0, tiled=True)  68.2 us
  transfers between devices with their start and end apart: 18, of which 17 were waited for; matrix products, arithmetic and copies ran while one was open for 15% of the time, Pallas kernels for 0%

commit v1 on v0

--- a/solution.py
+++ b/solution.py
@@ -223,17 +223,20 @@
         lax.psum_scatter(grad_out, "wide", scatter_dimension=1, tiled=True),
     )
     small_sums = lax.psum(
-        (
-            grad_gain_one,
-            grad_gain_two,
-            jnp.sum(grad_resid, axis=0),
-            jnp.sum(grad_half, axis=0),
-            grad_dim,
-            place_part(sum_query, b_query.shape[0], head_index * local_hd),
-            place_part(sum_value, b_value.shape[0], head_index * local_hd),
-            bias_up_term,
+        lax.psum(
+            (
+                grad_gain_one,
+                grad_gain_two,
+                jnp.sum(grad_resid, axis=0),
+                jnp.sum(grad_half, axis=0),
+                grad_dim,
+                place_part(sum_query, b_query.shape[0], head_index * local_hd),
+                place_part(sum_value, b_value.shape[0], head_index * local_hd),
+                bias_up_term,
+            ),
+            "heads",
         ),
-        ("wide", "heads"),
+        "wide",
     )
     (
         gain_one_sum,

time: 1300 us -> 1300 us (level)
  waiting for transfers between devices: 912 us -> 884 us
  blocking collectives: 41.1 us -> 68.6 us
    psum x0 -> x1, blocking collectives: none -> 60.9 us  [shards(): lax.psum(lax.psum((grad_gain_one, grad_gain_two, jnp.sum(grad_resid, axis...]
    psum x1, blocking collectives: 41.1 us -> 7.67 us  [shards(): lax.psum((grad_gain_one, grad_gain_two, jnp.sum(grad_resid, axis=0), jnp....]
    reduce_scatter x1, waiting for transfers between devices: 19.7 us -> 0.01 us  [shards(): lax.psum_scatter(grad_up, 'wide', scatter_dimension=0, tiled=True)]
  transfers between devices with their start and end apart: 18 -> 18, of which waited for: 17 -> 16; matrix products, arithmetic and copies ran while one was open for 15% -> 15% of each run, Pallas kernels for 0% -> 0%
where the time goes in v1:
time: 1300 us; the launch traced here: 1290 us
  waiting for transfers between devices  884 us (68%)
  matrix products  195 us (15%)
  local copies, waits for them, and re-layouts  70.2 us (5%)
  blocking collectives  68.6 us (5%)
  other arithmetic  53 us (4%)
  between operations  15 us (1%)
    reduce_scatter x1, waiting for transfers between devices, shards(): lax.psum_scatter(dot_plain(attended, out_full), 'heads', scatter_dimensio...  113 us
    reduce_scatter x1, waiting for transfers between devices, shards(): lax.psum_scatter(grad_key, 'wide', scatter_dimension=0, tiled=True)  70.5 us
    reduce_scatter x1, waiting for transfers between devices, shards(): lax.psum_scatter(grad_out, 'wide', scatter_dimension=1, tiled=True)  70.5 us
    reduce_scatter x1, waiting for transfers between devices, shards(): lax.psum_scatter(grad_value, 'wide', scatter_dimension=0, tiled=True)  70.1 us
    reduce_scatter x1, waiting for transfers between devices, shards(): lax.psum_scatter(grad_query, 'wide', scatter_dimension=0, tiled=True)  70.1 us
    all_gather x1, waiting for transfers between devices, shards(): normed_two = lax.all_gather(normed_half, 'heads', axis=0, tiled=True)  69.6 us
    all_gather x1, waiting for transfers between devices, shards(): grad_branch = lax.all_gather(branch_half, 'heads', axis=0, tiled=True)  68.2 us
    reduce_scatter x1, waiting for transfers between devices, shards(): lax.psum_scatter(dot_plain(activated, down_full).astype(jnp.bfloat16), 'h...  63 us
  transfers between devices with their start and end apart: 18, of which 16 were waited for; matrix products, arithmetic and copies ran while one was open for 15% of the time, Pallas kernels for 0%

profile of v1, /device:TPU:0, one launch (start us, length us, event | category | flops | bytes accessed | tf_op | source)
XLA Modules:
  0.0 1287.5 jit_solution(2870112703341335290)
XLA Ops:
  12.3 3.6 multiply_reduce_fusion
  16.3 36.5 %all-gather.9.cloned.1.call-done = bf16[1280,640]{1,0:T(8,128)(2,1)} async-done(((bf16[80,640]{1,0:T(8,128)(2,1)}), bf16[1280,640]{1,0:T(8,128)(2,1)}) %all-gather.9.cloned.1.call-update) | async-done | bytes 1638416 | tf_op jit(solution)/shard_map/all_gather | solution.py:101
  52.9 7.4 add_convert_fusion.2
  60.2 33.6 %all-gather.11.cloned.1.call-done = bf16[1280,640]{1,0:T(8,128)(2,1)} async-done(((bf16[80,640]{1,0:T(8,128)(2,1)}), bf16[1280,640]{1,0:T(8,128)(2,1)}) %all-gather.11.cloned.1.call-update) | async-done | bytes 1638416 | tf_op jit(solution)/shard_map/all_gather | solution.py:99
  93.9 9.7 convolution_add_fusion
  103.5 31.4 %all-gather.13.cloned.1.call-done = bf16[1280,640]{1,0:T(8,128)(2,1)} async-done(((bf16[80,640]{1,0:T(8,128)(2,1)}), bf16[1280,640]{1,0:T(8,128)(2,1)}) %all-gather.13.cloned.1.call-update) | async-done | bytes 1638416 | tf_op jit(solution)/shard_map/all_gather | solution.py:100
  134.9 9.3 convolution_convert_fusion.3
  144.2 5.2 reshape.228
  149.4 6.3 copy.50
  155.7 5.2 reshape.230
  160.9 6.1 copy.49
  167.0 9.4 reshape.229
  176.4 8.3 copy.47
  184.7 4.5 select_reduce_fusion
  189.2 2.4 fusion
  192.8 2.4 convert_bitcast_fusion.1
  197.0 10.0 fusion.42
  207.7 7.6 convert_element_type.111
  215.4 112.8 %reduce-scatter.11.cloned.1.call-done = f32[1024,1280]{1,0:T(8,128)} async-done(((f32[2048,1280]{1,0:T(8,128)}), f32[1024,1280]{1,0:T(8,128)}) %reduce-scatter.11.cloned.1.call-update) | async-done | bytes 5242896 | tf_op jit(solution)/shard_map/reduce_scatter | solution.py:129
  328.2 5.8 multiply_reduce_fusion.3
  334.0 2.4 copy-done.1
  336.3 2.0 multiply_convert_fusion.3
  339.2 30.9 %all-gather.19.cloned.1.call-done = bf16[1280,640]{1,0:T(8,128)(2,1)} async-done(((bf16[80,640]{1,0:T(8,128)(2,1)}), bf16[1280,640]{1,0:T(8,128)(2,1)}) %all-gather.19.cloned.1.call-update) | async-done | bytes 1638416 | tf_op jit(solution)/shard_map/all_gather | solution.py:126
  370.1 69.6 %all-gather.17.cloned.1.call-done = bf16[2048,1280]{1,0:T(8,128)(2,1)} async-done(((bf16[1024,1280]{1,0:T(8,128)(2,1)}), bf16[2048,1280]{1,0:T(8,128)(2,1)}) %all-gather.17.cloned.1.call-update) | async-done | bytes 5242896 | tf_op jit(solution)/shard_map/all_gather | solution.py:134
  439.8 9.5 fusion.64
  449.3 32.6 %all-gather.21.cloned.1.call-done = bf16[640,1280]{0,1:T(8,128)(2,1)} async-done(((bf16[640,80]{0,1:T(8,128)(2,1)}), bf16[640,1280]{0,1:T(8,128)(2,1)}) %all-gather.21.cloned.1.call-update) | async-done | bytes 1638416 | tf_op jit(solution)/shard_map/all_gather | solution.py:127
  481.9 10.0 convert_reduce_fusion.1
  493.4 6.0 convolution_convert_fusion
  500.8 10.5 convolution_convert_fusion.1
  511.3 52.8 %reduce-scatter.15.cloned.1.call-done = bf16[1024,1280]{1,0:T(8,128)(2,1)} async-done(((bf16[2048,1280]{1,0:T(8,128)(2,1)}), bf16[1024,1280]{1,0:T(8,128)(2,1)}) %reduce-scatter.15.cloned.1.call-update) | async-done | bytes 2621456 | tf_op jit(solution)/shard_map/reduce_scatter | solution.py:156
  564.1 5.0 fusion.13
  569.2 63.0 %reduce-scatter.13.cloned.1.call-done = bf16[1024,1280]{1,0:T(8,128)(2,1)} async-done(((bf16[2048,1280]{1,0:T(8,128)(2,1)}), bf16[1024,1280]{1,0:T(8,128)(2,1)}) %reduce-scatter.13.cloned.1.call-update) | async-done | bytes 2621456 | tf_op jit(solution)/shard_map/reduce_scatter | solution.py:137
  632.1 6.8 fusion.62
  638.9 2.4 copy-done.2
  641.3 1.8 convert_element_type.129
  643.7 68.2 %all-gather.23.cloned.1.call-done = bf16[2048,1280]{1,0:T(8,128)(2,1)} async-done(((bf16[1024,1280]{1,0:T(8,128)(2,1)}), bf16[2048,1280]{1,0:T(8,128)(2,1)}) %all-gather.23.cloned.1.call-update) | async-done | bytes 5242896 | tf_op jit(solution)/shard_map/all_gather | solution.py:171
  711.9 7.2 convolution_convert_fusion.2
  719.2 5.2 reshape.231
  724.4 6.1 copy.54
  730.5 8.1 convert_reduce_fusion.2
  738.5 10.1 multiply_reduce_fusion.1
  748.6 5.4 multiply_convert_fusion.1
  754.1 1.8 convert_reduce_fusion.3
  755.9 3.1 convert_bitcast_fusion
  759.0 1.7 copy.63
  764.1 7.8 fusion.34
  771.9 8.1 fusion.38
  780.0 11.3 add_convert_fusion
  791.4 9.4 fusion.65
  801.3 10.3 fusion.60
  811.7 9.2 fusion.40
  821.2 10.1 fusion.36
  831.4 9.8 fusion.32
  841.5 9.1 fusion.29
  851.7 5.5 reduce-scatter.17.cloned.1.call-done
  857.2 5.0 fusion.19
  862.2 7.7 all-reduce.1
  869.9 60.9 %all-reduce = (f32[1280]{0:T(1024)}, f32[1280]{0:T(1024)}, f32[1280]{0:T(1024)}, f32[1280]{0:T(1024)}, f32[1280]{0:T(1024)}, /*index=5*/f32[80]{0:T(128)}, f32[1280]{0:T(1024)}, f32[1280]{0:T(1024)}) all-reduce(f32[1280]{0:T(1024)S(1)} %get-tuple-element.28, ...), channel_id=1, replica_groups=mesh['wide'=16,'heads'=2] {'wide'}, use_global_device_ids=true, to_apply=%region_20.21 | all-reduce | flops 9040 | bytes 72320 | tf_op jit(solution)/shard_map/psum | solution.py:225
  930.8 6.4 fusion.15
  937.3 62.0 %reduce-scatter.29.cloned.1.call-done = f32[640,80]{0,1:T(8,128)} async-done(((f32[640,1280]{0,1:T(8,128)}), f32[640,80]{0,1:T(8,128)}) %reduce-scatter.29.cloned.1.call-update) | async-done | bytes 204816 | tf_op jit(solution)/shard_map/reduce_scatter | solution.py:217
  999.2 70.5 %reduce-scatter.25.cloned.1.call-done = f32[640,80]{0,1:T(8,128)} async-done(((f32[640,1280]{0,1:T(8,128)}), f32[640,80]{0,1:T(8,128)}) %reduce-scatter.25.cloned.1.call-update) | async-done | bytes 204816 | tf_op jit(solution)/shard_map/reduce_scatter | solution.py:223
  1069.7 70.1 %reduce-scatter.19.cloned.1.call-done = f32[80,640]{1,0:T(8,128)} async-done(((f32[1280,640]{1,0:T(8,128)}), f32[80,640]{1,0:T(8,128)}) %reduce-scatter.19.cloned.1.call-update) | async-done | bytes 204816 | tf_op jit(solution)/shard_map/reduce_scatter | solution.py:220
  1139.8 70.5 %reduce-scatter.21.cloned.1.call-done = f32[80,640]{1,0:T(8,128)} async-done(((f32[1280,640]{1,0:T(8,128)}), f32[80,640]{1,0:T(8,128)}) %reduce-scatter.21.cloned.1.call-update) | async-done | bytes 204816 | tf_op jit(solution)/shard_map/reduce_scatter | solution.py:221
  1210.4 70.1 %reduce-scatter.23.cloned.1.call-done = f32[80,640]{1,0:T(8,128)} async-done(((f32[1280,640]{1,0:T(8,128)}), f32[80,640]{1,0:T(8,128)}) %reduce-scatter.23.cloned.1.call-update) | async-done | bytes 204816 | tf_op jit(solution)/shard_map/reduce_scatter | solution.py:222
  (131 shorter events, 19.1 us)
Async XLA Ops:
  7.2 8.8 copy-start.17
  7.2 45.7 %copy-start.15 = (f32[1280]{0:T(1024)S(1)}, f32[1280]{0:T(1024)}, u32[]{:S(2)}) copy-start(f32[1280]{0:T(1024)} %param.32) | copy-start | bytes 15364
  7.2 45.7 %all-gather.9.cloned.1.call-start = ((), (), s32[]{:S(2)}) async-start(), calls=%async_computation.10 | async-start | bytes 1740800 | tf_op jit(solution)/shard_map/all_gather | solution.py:101
  7.9 85.9 %all-gather.11.cloned.1.call-start = ((), (), s32[]{:S(2)}) async-start(), calls=%async_computation.11 | async-start | bytes 1740800 | tf_op jit(solution)/shard_map/all_gather | solution.py:99
  8.7 126.2 %all-gather.13.cloned.1.call-start = ((), (), s32[]{:S(2)}) async-start(), calls=%async_computation.12 | async-start | bytes 1740800 | tf_op jit(solution)/shard_map/all_gather | solution.py:100
  9.4 187.6 %all-gather.15.cloned.1.call-start = ((), (), s32[]{:S(2)}) async-start(), calls=%async_computation.13 | async-start | bytes 1740800 | tf_op jit(solution)/shard_map/all_gather | solution.py:102
  10.0 318.2 %reduce-scatter.11.cloned.1.call-start = ((), (), s32[]{:S(2)}) async-start(), calls=%async_computation.14 | async-start | bytes 15728640 | tf_op jit(solution)/shard_map/reduce_scatter | solution.py:129
  15.9 119.0 %copy-start.21 = (f32[2048]{0:T(1024)}, f32[2048]{0:T(1024)S(1)}, u32[]{:S(2)}) copy-start(f32[2048]{0:T(1024)S(1)} %add_rsqrt_fusion) | copy-start | bytes 24580
  149.4 6.3 copy-start.12
  167.0 17.7 %copy-start.3 = (bf16[16,128,8,80]{1,3,2,0:T(8,128)(2,1)}, bf16[16,128,8,80]{1,3,2,0:T(8,128)(2,1)S(1)}, u32[]{:S(2)}) copy-start(bf16[16,128,8,80]{1,3,2,0:T(8,128)(2,1)S(1)} %copy.49) | copy-start | bytes 7864324
  189.2 6.1 copy-start
  189.2 3.7 copy-start.7
  197.0 10.1 copy-start.9
  207.1 163.1 %all-gather.19.cloned.1.call-start = ((), (), s32[]{:S(2)}) async-start(), calls=%async_computation.16 | async-start | bytes 1740800 | tf_op jit(solution)/shard_map/all_gather | solution.py:126
  207.7 120.5 %copy-start.19 = (f32[1280]{0:T(1024)S(1)}, f32[1280]{0:T(1024)}, u32[]{:S(2)}) copy-start(f32[1280]{0:T(1024)} %param.28) | copy-start | bytes 15364
  207.7 232.1 %all-gather.17.cloned.1.call-start = ((), (), s32[]{:S(2)}) async-start(), calls=%async_computation.15 | async-start | bytes 7864320 | tf_op jit(solution)/shard_map/all_gather | solution.py:134
  215.4 121.0 %copy-start.14 = (f32[1280]{0:T(1024)S(1)}, f32[1280]{0:T(1024)}, u32[]{:S(2)}) copy-start(f32[1280]{0:T(1024)} %param.33) | copy-start | bytes 15364
  334.0 2.4 copy-start.1
  336.3 2.8 copy-start.23
  338.3 143.5 %all-gather.21.cloned.1.call-start = ((), (), s32[]{:S(2)}) async-start(), calls=%async_computation.17 | async-start | bytes 1740800 | tf_op jit(solution)/shard_map/all_gather | solution.py:127
  339.1 225.0 %reduce-scatter.15.cloned.1.call-start = ((), (), s32[]{:S(2)}) async-start(), calls=%async_computation.19 | async-start | bytes 7864320 | tf_op jit(solution)/shard_map/reduce_scatter | solution.py:156
  449.3 44.1 %copy-start.26 = (bf16[1280,640]{1,0:T(8,128)(2,1)S(1)}, bf16[1280,640]{1,0:T(8,128)(2,1)}, u32[]{:S(2)}) copy-start(bf16[1280,640]{1,0:T(8,128)(2,1)} %all-gather.19.cloned.1.call-done) | copy-start | bytes 4915204
  491.9 1.5 copy-start.29
  499.4 1.4 copy-start.27
  499.4 132.7 %reduce-scatter.13.cloned.1.call-start = ((), (), s32[]{:S(2)}) async-start(), calls=%async_computation.18 | async-start | bytes 7864320 | tf_op jit(solution)/shard_map/reduce_scatter | solution.py:137
  511.3 120.8 %copy-start.20 = (f32[1280]{0:T(1024)S(1)}, f32[1280]{0:T(1024)}, u32[]{:S(2)}) copy-start(f32[1280]{0:T(1024)} %param.30) | copy-start | bytes 15364
  511.3 200.6 %all-gather.23.cloned.1.call-start = ((), (), s32[]{:S(2)}) async-start(), calls=%async_computation.20 | async-start | bytes 7864320 | tf_op jit(solution)/shard_map/all_gather | solution.py:171
  564.1 68.0 %copy-start.8 = (bf16[1024,1280]{1,0:T(8,128)(2,1)S(1)}, bf16[1024,1280]{1,0:T(8,128)(2,1)}, u32[]{:S(2)}) copy-start(bf16[1024,1280]{1,0:T(8,128)(2,1)} %reduce-scatter.15.cloned.1.call-done) | copy-start | bytes 7864324
  638.9 2.4 copy-start.2
  643.2 214.0 %reduce-scatter.17.cloned.1.call-start = ((), (), s32[]{:S(2)}) async-start(), calls=%async_computation.21 | async-start | bytes 7864320 | tf_op jit(solution)/shard_map/reduce_scatter | solution.py:210
  730.5 18.2 %slice-start = ((s8[8388608]{0:T(1024)(128)(4,1)}), s8[4194304]{0:T(1024)(128)(4,1)S(1)}, s32[]{:S(2)}) async-start(s8[8388608]{0:T(1024)(128)(4,1)} %bitcast.78), calls=%async_computation.28 | async-start | bytes 8388608
  730.5 23.6 %slice-start.2 = ((s8[5242880]{0:T(1024)(128)(4,1)}), s8[4194304]{0:T(1024)(128)(4,1)S(1)}, s32[]{:S(2)}) async-start(s8[5242880]{0:T(1024)(128)(4,1)} %bitcast.80), calls=%async_computation.30 | async-start | bytes 8388608
  738.5 10.1 slice-start.1
  738.5 15.5 %slice-start.3 = ((s8[5242880]{0:T(1024)(128)(4,1)}), s8[1048576]{0:T(1024)(128)(4,1)S(1)}, s32[]{:S(2)}) async-start(s8[5242880]{0:T(1024)(128)(4,1)} %bitcast.80), calls=%async_computation.31 | async-start | bytes 2097152
  748.6 5.4 copy-start.4
  755.9 3.1 copy-start.6
  760.7 3.4 copy-start.25
  762.4 9.5 copy-start.10
  764.1 7.8 copy-start.11
  764.1 7.8 copy-start.24
  771.9 8.1 copy-start.13
  791.4 145.9 %reduce-scatter.27.cloned.1.call-start = ((), (), s32[]{:S(2)}) async-start(), calls=%async_computation.26 | async-start | bytes 3481600 | tf_op jit(solution)/shard_map/reduce_scatter | solution.py:216
  800.9 198.3 %reduce-scatter.29.cloned.1.call-start = ((), (), s32[]{:S(2)}) async-start(), calls=%async_computation.27 | async-start | bytes 3481600 | tf_op jit(solution)/shard_map/reduce_scatter | solution.py:217
  811.6 9.6 copy-start.16
  811.7 9.6 copy-start.22
  811.7 258.1 %reduce-scatter.25.cloned.1.call-start = ((), (), s32[]{:S(2)}) async-start(), calls=%async_computation.25 | async-start | bytes 3481600 | tf_op jit(solution)/shard_map/reduce_scatter | solution.py:223
  821.0 318.8 %reduce-scatter.19.cloned.1.call-start = ((), (), s32[]{:S(2)}) async-start(), calls=%async_computation.22 | async-start | bytes 3481600 | tf_op jit(solution)/shard_map/reduce_scatter | solution.py:220
  831.4 379.0 %reduce-scatter.21.cloned.1.call-start = ((), (), s32[]{:S(2)}) async-start(), calls=%async_computation.23 | async-start | bytes 3481600 | tf_op jit(solution)/shard_map/reduce_scatter | solution.py:221
  841.2 9.4 copy-start.18
  841.2 10.5 copy-start.28
  841.2 439.2 %reduce-scatter.23.cloned.1.call-start = ((), (), s32[]{:S(2)}) async-start(), calls=%async_computation.24 | async-start | bytes 3481600 | tf_op jit(solution)/shard_map/reduce_scatter | solution.py:222
  857.2 73.6 %copy-start.5 = (bf16[1024,1280]{1,0:T(8,128)(2,1)S(1)}, bf16[1024,1280]{1,0:T(8,128)(2,1)}, u32[]{:S(2)}) copy-start(bf16[1024,1280]{1,0:T(8,128)(2,1)} %reduce-scatter.17.cloned.1.call-done) | copy-start | bytes 7864324
Sparse Core Ops, SparseCore 0:
  10.2 42.6 all-gather.8
  55.0 38.8 all-gather.10
  96.1 38.8 all-gather.12
  136.9 38.8 all-gather.14
  207.2 120.9 reduce-scatter.10
  330.2 39.8 all-gather.18
  372.2 67.4 all-gather.16
  441.9 39.9 all-gather.20
  499.5 64.5 reduce-scatter.14
  566.4 65.6 reduce-scatter.12
  643.3 68.5 all-gather.22
  791.5 65.6 reduce-scatter.16
  862.1 67.1 reduce-scatter.26
  933.5 65.6 reduce-scatter.28
  1004.0 65.7 reduce-scatter.24
  1074.0 65.7 reduce-scatter.18
  1144.5 65.7 reduce-scatter.20
  1214.6 65.7 reduce-scatter.22
